TPU v7x, 512 devices: a whole 4x4x16 slice. The times are simulated.
512 devices in a mesh: prow: 16 (over y, x), pcol: 32 (over z, core).
Axes of the slice: x: 4, y: 4, z: 16, core: 2. Of those that a mesh axis runs over, the one named last changes fastest.
Arguments:
- matrix: float32 [4, 16, 256, 2, 32, 256], P(None, 'prow', None, None, 'pcol'), may hold values from -6 to 6
- pivots: int32 [2, 256], replicated, may hold values from 256 to 16383, as said below
- inverse_blocks: float32 [2, 256, 256], replicated, may hold values from -1 to 1
Outputs:
- factored: float32 [4, 16, 256, 2, 32, 256], P(None, 'prow', None, None, 'pcol')
Inputs may be any that keep to these rules, and one draw needn't show every extreme that they name: Entries of pivots[0] lie in 256 to 16383, entries of pivots[1] in 512 to 16383; the entries of one panel are distinct.
All inputs are finite; a program needn't handle non-finite values.
Results may differ from a plain program's by a relative error of at most 0.00013.
Values sent between devices are 32-bit elements; how exact they have to be, the bound alone decides.
A program may use at most 64 MiB of HBM per device.

v0:
```python
import jax
import jax.numpy as jnp
from jax import lax
from jax.sharding import PartitionSpec as P


def spread(block, axis, source):
    block = jnp.where(lax.axis_index(axis) == source, block, jnp.zeros_like(block))
    return lax.psum(block, axis)


def product(left, right_side):
    return jnp.dot(
        left, right_side, precision=lax.Precision.HIGHEST, preferred_element_type=jnp.float32
    )


def shards(matrix, pivots, inverse_blocks):
    full_shape = matrix.shape
    row_blocks = full_shape[0]
    width = full_shape[2]
    col_blocks = full_shape[3]
    proc_rows = lax.axis_size("prow")
    proc_cols = lax.axis_size("pcol")
    me_row = lax.axis_index("prow")
    me_col = lax.axis_index("pcol")
    local_rows = row_blocks * width
    local_block = matrix.reshape(local_rows, col_blocks * width)
    row_global = jnp.arange(local_rows) // width * proc_rows + me_row
    col_global = jnp.arange(col_blocks * width) // width * proc_cols + me_col
    identity = jnp.eye(width, dtype=jnp.float32)
    for section in range(2):
        root_row = section % proc_rows
        root_col = section % proc_cols
        row_start = section // proc_rows * width
        col_start = section // proc_cols * width
        pivot_list = pivots[section]
        global_block = pivot_list // width
        owned_rows = global_block % proc_rows == me_row
        local_spot = global_block // proc_rows * width + pivot_list % width
        picked = jnp.where(owned_rows[:, None], local_block[local_spot], 0.0)
        current = local_block[row_start : row_start + width]
        pivot_rows = lax.psum(picked, "prow")
        old_rows = spread(current, "prow", root_row)
        local_block = local_block.at[row_start : row_start + width].set(
            jnp.where(me_row == root_row, pivot_rows, current)
        )
        target = jnp.where(owned_rows, local_spot, local_rows)
        local_block = local_block.at[target].set(old_rows, mode="drop")
        packed = inverse_blocks[section]
        upper_inv = jnp.triu(packed)
        lower_inv = jnp.tril(packed, -1) + identity
        column = spread(local_block[:, col_start : col_start + width], "pcol", root_col)
        below_rows = row_global > section
        lower_panel = jnp.where(below_rows[:, None], product(column, upper_inv), 0.0)
        right_cols = col_global > section
        upper_rows = spread(
            product(lower_inv, local_block[row_start : row_start + width]), "prow", root_row
        )
        upper_rows = jnp.where(right_cols[None, :], upper_rows, 0.0)
        local_block = local_block - product(lower_panel, upper_rows)
        new_column = jnp.where(below_rows[:, None], lower_panel, column)
        old_column = local_block[:, col_start : col_start + width]
        local_block = local_block.at[:, col_start : col_start + width].set(
            jnp.where(me_col == root_col, new_column, old_column)
        )
        current = local_block[row_start : row_start + width]
        solved = jnp.where(right_cols[None, :], upper_rows, current)
        local_block = local_block.at[row_start : row_start + width].set(
            jnp.where(me_row == root_row, solved, current)
        )
    return local_block.reshape(full_shape)


def solution(mesh):
    return jax.shard_map(
        shards,
        mesh=mesh,
        in_specs=(P(None, "prow", None, None, "pcol", None), P(), P()),
        out_specs=P(None, "prow", None, None, "pcol", None),
        check_vma=False,
    )
```

profile of v0, /device:TPU:32, one launch (start us, length us, event | category | flops | bytes accessed | tf_op | source)
XLA Modules:
  0.0 958.9 jit_solution(581236438415859712)
XLA Ops:
  8.1 2.7 slice_reduce_fusion
  10.8 9.0 reduce.17
  19.8 1.8 copy.6
  24.5 122.1 %all-reduce.19.cloned.1.call-done = (f32[256,512]{1,0:T(8,128)}, f32[256,512]{1,0:T(8,128)}) async-done(((f32[256,512]{1,0:T(8,128)}, f32[256,512]{1,0:T(8,128)}), (f32[256,512]{1,0:T(8,128)}, f32[256,512]{1,0:T(8,128)})) %all-reduce.19.cloned.1.call-update) | async-done | bytes 1048592 | tf_op jit(solution)/shard_map/psum | solution.py:43
  146.6 1.1 select_dynamic-update-slice_fusion.1
  147.7 2.7 scatter_fusion
  150.4 1.1 slice_select_fusion.1
  151.9 1.5 convolution_select_fusion.3
  154.3 203.6 %all-reduce.9.cloned.1.call-done = f32[1024,256]{1,0:T(8,128)} async-done(((f32[1024,256]{1,0:T(8,128)}), f32[1024,256]{1,0:T(8,128)}) %all-reduce.9.cloned.1.call-update) | async-done | bytes 1048592 | tf_op jit(solution)/shard_map/psum | solution.py:9
  358.0 2.3 convolution_select_fusion.1
  360.3 119.4 %all-reduce.11.cloned.1.call-done = f32[256,512]{1,0:T(8,128)} async-done(((f32[256,512]{1,0:T(8,128)}), f32[256,512]{1,0:T(8,128)}) %all-reduce.11.cloned.1.call-update) | async-done | bytes 524304 | tf_op jit(solution)/shard_map/psum | solution.py:9
  479.7 3.7 convolution_subtract_fusion.1
  483.4 1.0 fusion
  487.4 117.5 %all-reduce.17.cloned.1.call-done = (f32[256,512]{1,0:T(8,128)}, f32[256,512]{1,0:T(8,128)}) async-done(((f32[256,512]{1,0:T(8,128)}, f32[256,512]{1,0:T(8,128)}), (f32[256,512]{1,0:T(8,128)}, f32[256,512]{1,0:T(8,128)})) %all-reduce.17.cloned.1.call-update) | async-done | bytes 1048592 | tf_op jit(solution)/shard_map/psum | solution.py:43
  605.0 2.7 scatter_fusion.1
  607.7 1.1 slice_select_fusion
  608.9 1.5 convolution_select_fusion.2
  610.4 205.8 %all-reduce.13.cloned.1.call-done = f32[1024,256]{1,0:T(8,128)} async-done(((f32[1024,256]{1,0:T(8,128)}), f32[1024,256]{1,0:T(8,128)}) %all-reduce.13.cloned.1.call-update) | async-done | bytes 1048592 | tf_op jit(solution)/shard_map/psum | solution.py:9
  816.2 2.3 convolution_select_fusion
  818.6 119.3 %all-reduce.15.cloned.1.call-done = f32[256,512]{1,0:T(8,128)} async-done(((f32[256,512]{1,0:T(8,128)}), f32[256,512]{1,0:T(8,128)}) %all-reduce.15.cloned.1.call-update) | async-done | bytes 524304 | tf_op jit(solution)/shard_map/psum | solution.py:9
  937.8 4.3 convolution_subtract_fusion
  942.1 3.2 fusion.1
  945.4 1.9 fusion.2
  947.3 4.7 reshape.648
  (50 shorter events, 8.8 us)
Async XLA Ops:
  6.5 140.1 %all-reduce.19.cloned.1.call-start = ((), (), s32[]{:S(2)}) async-start(), calls=%async_computation.5 | async-start | bytes 2097152 | tf_op jit(solution)/shard_map/psum | solution.py:43
  24.4 333.5 %all-reduce.9.cloned.1.call-start = ((), (), s32[]{:S(2)}) async-start(), calls=%async_computation | async-start | bytes 2097152 | tf_op jit(solution)/shard_map/psum | solution.py:9
  150.4 2.9 copy-start
  150.4 1.4 copy-start.5
  151.6 328.1 %all-reduce.11.cloned.1.call-start = ((), (), s32[]{:S(2)}) async-start(), calls=%async_computation.1 | async-start | bytes 1048576 | tf_op jit(solution)/shard_map/psum | solution.py:9
  153.4 451.5 %all-reduce.17.cloned.1.call-start = ((), (), s32[]{:S(2)}) async-start(), calls=%async_computation.4 | async-start | bytes 2097152 | tf_op jit(solution)/shard_map/psum | solution.py:43
  479.7 3.7 copy-start.1
  483.4 1.0 copy-start.3
  487.4 328.8 %all-reduce.13.cloned.1.call-start = ((), (), s32[]{:S(2)}) async-start(), calls=%async_computation.2 | async-start | bytes 2097152 | tf_op jit(solution)/shard_map/psum | solution.py:9
  607.7 1.2 copy-start.6
  608.8 329.0 %all-reduce.15.cloned.1.call-start = ((), (), s32[]{:S(2)}) async-start(), calls=%async_computation.3 | async-start | bytes 1048576 | tf_op jit(solution)/shard_map/psum | solution.py:9
  937.8 4.3 copy-start.2
  942.1 3.2 copy-start.4
Sparse Core Ops, SparseCore 0:
  24.5 121.9 all-reduce.18
  151.7 206.1 all-reduce.8
  361.5 118.1 all-reduce.10
  487.5 117.3 all-reduce.16
  608.9 207.2 all-reduce.12
  819.6 118.1 all-reduce.14
where the time goes:
time: 960 us; the launch traced here: 959 us
  waiting for transfers between devices  888 us (92%)
  other arithmetic  23.9 us (2%)
  local copies, waits for them, and re-layouts  17.5 us (2%)
  matrix products  15.6 us (2%)
  between operations  13.7 us (1%)
    psum x4, waiting for transfers between devices, spread(): return lax.psum(block, axis)  648 us
    psum x2, waiting for transfers between devices, shards(): pivot_rows = lax.psum(picked, 'prow')  240 us
  transfers between devices with their start and end apart: 6, of which 6 were waited for; matrix products, arithmetic and copies ran while one was open for 1% of the time, Pallas kernels for 0%

commit v1 on v0

v1 whole, which is shorter than its diff:
```python
import functools

import jax
import jax.numpy as jnp
from jax import lax
from jax.experimental import pallas as pl
from jax.experimental.pallas import tpu as pltpu
from jax.sharding import PartitionSpec as P

F32, BF16 = jnp.float32, jnp.bfloat16
CHUNKS = 20


def mul(left, right):
    return jnp.dot(left, right, preferred_element_type=F32)


def parts2(x):
    high = x.astype(BF16)
    return high, (x - high.astype(F32)).astype(BF16)


def parts3(x):
    high = x.astype(BF16)
    rest = x - high.astype(F32)
    mid = rest.astype(BF16)
    return high, mid, (rest - mid.astype(F32)).astype(BF16)


def product(left, right):
    lh, ll = parts2(left)
    rh, rl = parts2(right)
    return mul(lh, rh) + (mul(lh, rl) + mul(ll, rh))


def kernel(
    sizes, x, piv, pivt, inv, out,
    a, s0, s1, s2, picks, rs, ag, panel, u, uh, ul, old0, old1, old2,
    in_sem, out_sem, rs_send, rs_recv, old_send, old_recv, ag_send, ag_recv,
    z_send, z_send2, z_recv, sib_send, sib_recv,
):
    rb, cb, nb, np_, nz = sizes
    rows, width, slots = rb * nb, cb * nb, 2 * nb
    ch, co = slots // np_, nb // np_
    height = nb + rows
    piece = height // CHUNKS
    me = lax.axis_index("prow")
    col = lax.axis_index("pcol")
    z, core = col // 2, col % 2

    def at_row(r):
        return {"prow": r, "pcol": col}

    def at_col(zz, cc):
        return {"prow": me, "pcol": zz * 2 + cc}

    def load(r, c):
        return pltpu.make_async_copy(
            x.at[r, 0, :, c, 0, :],
            a.at[pl.ds(r * nb, nb), pl.ds(c * nb, nb)],
            in_sem.at[r * cb + c],
        )

    for r in range(rb):
        for c in range(cb):
            load(r, c).start()

    barrier = pltpu.get_barrier_semaphore()

    def greet(d, carry):
        pl.semaphore_signal(barrier, inc=1, device_id=at_row((me + d) % np_))
        return carry

    lax.fori_loop(1, np_, greet, 0)
    for zz, cc in (((z + 1) % nz, core), ((z + nz - 1) % nz, core), (z, 1 - core)):
        pl.semaphore_signal(barrier, inc=1, device_id=at_col(zz, cc))

    p0r, p1r = piv[0:1, :], piv[1:2, :]
    p0c, p1c = pivt[:, 0:1], pivt[:, 1:2]
    lane = lax.broadcasted_iota(jnp.int32, (nb, nb), 1)
    sub = lax.broadcasted_iota(jnp.int32, (nb, nb), 0)
    same = p1c == p0r
    back = jnp.max(jnp.where(same, lane, -1), axis=1, keepdims=True)
    src0, src1 = p0c, jnp.where(back >= 0, back, p1c)
    hit = jnp.max(jnp.where(p0r == sub + nb, p1c, -1), axis=0, keepdims=True)
    gone = jnp.max(jnp.where(same, 1, 0), axis=0, keepdims=True)
    dst0 = jnp.where(hit >= 0, hit, jnp.where(gone > 0, -1, p0r))
    up = jnp.max(jnp.where(p0c == lane + nb, 1, 0), axis=0, keepdims=True)
    dst1 = jnp.where(up > 0, -1, p1r)

    for r in range(rb):
        for c in range(cb):
            load(r, c).wait()

    def split(r, carry):
        at = pl.ds(pl.multiple_of(r * nb, nb), nb)
        h, m, l = parts3(a[at, :])
        s0[at, :], s1[at, :], s2[at, :] = h, m, l
        return carry

    lax.fori_loop(0, rb, split, 0)
    for k, src in ((0, src0), (1, src1)):
        total = jnp.zeros((nb, width), F32)
        for r in range(rb):
            here = (r * np_ + me) * nb + lane
            pick = (src == here).astype(F32).astype(BF16)
            at = pl.ds(r * nb, nb)
            total = total + (mul(pick, s0[at, :]) + mul(pick, s1[at, :]) + mul(pick, s2[at, :]))
        picks[pl.ds(k * nb, nb), :] = total

    pl.semaphore_wait(barrier, np_ - 1 + 3)

    def rs_copy(d):
        to = (me + d) % np_
        return pltpu.make_async_remote_copy(
            picks.at[pl.ds(pl.multiple_of(to * ch, ch), ch), :], rs.at[me],
            rs_send.at[d], rs_recv.at[d], device_id=at_row(to),
        )

    def old_copy(k, d):
        to = (me + d) % np_
        return pltpu.make_async_remote_copy(
            a.at[pl.ds(pl.multiple_of(to * co, co), co), :],
            ag.at[to, pl.ds(ch + k * co, co), :],
            old_send.at[d], old_recv.at[k], device_id=at_row(to),
        )

    def ag_copy(d):
        return pltpu.make_async_remote_copy(
            ag.at[me], ag.at[me], ag_send.at[d], ag_recv.at[d], device_id=at_row((me + d) % np_),
        )

    def loop(low, high, body):
        def step(d, carry):
            body(d)
            return carry

        lax.fori_loop(low, high, step, 0)

    for k in range(2):
        @pl.when(me == k)
        def _():
            loop(1, np_, lambda d: old_copy(k, d).start())
            ag[me, pl.ds(ch + k * co, co), :] = a[pl.ds(pl.multiple_of(me * co, co), co), :]

    loop(1, np_, lambda d: rs_copy(d).start())
    ag[me, pl.ds(0, ch), :] = picks[pl.ds(pl.multiple_of(me * ch, ch), ch), :]

    def add(d):
        pltpu.make_async_remote_copy(
            rs.at[me], rs.at[(me + np_ - d) % np_], rs_send.at[d], rs_recv.at[d], device_id=at_row((me + d) % np_),
        ).wait_recv()
        ag[me, pl.ds(0, ch), :] = ag[me, pl.ds(0, ch), :] + rs[(me + np_ - d) % np_]

    loop(1, np_, add)
    for k in range(2):
        @pl.when(me != k)
        def _():
            pltpu.make_async_remote_copy(
                ag.at[me, pl.ds(ch, co), :], ag.at[me, pl.ds(ch + k * co, co), :],
                old_send.at[0], old_recv.at[k], device_id=at_row((me + 1) % np_),
            ).wait_recv()

    loop(1, np_, lambda d: ag_copy(d).start())

    def ag_wait(d):
        pltpu.make_async_remote_copy(
            ag.at[me], ag.at[(me + np_ - d) % np_], ag_send.at[d], ag_recv.at[d], device_id=at_row((me + d) % np_),
        ).wait_recv()

    loop(1, np_, ag_wait)
    for k in range(2):
        @pl.when(me == k)
        def _():
            loop(1, np_, lambda d: old_copy(k, d).wait_send())

    for k in range(2):
        at = pl.ds(k * nb, nb)
        h, m, l = parts3(ag[:, pl.ds(ch + k * co, co), :].reshape(nb, width))
        old0[at, :], old1[at, :], old2[at, :] = h, m, l

    def place(c):
        cs = pl.ds(c * nb, nb)

        def step(r):
            at = pl.ds(pl.multiple_of(r * nb, nb), nb)
            here = (r * np_ + me) * nb + sub
            total, moved = jnp.zeros((nb, nb), F32), jnp.zeros((nb, 1), F32)
            for k, dst in ((0, dst0), (1, dst1)):
                put = (dst == here).astype(F32)
                moved = jnp.maximum(moved, jnp.max(put, axis=1, keepdims=True))
                put = put.astype(BF16)
                ks = pl.ds(k * nb, nb)
                total = total + (mul(put, old0[ks, cs]) + mul(put, old1[ks, cs]) + mul(put, old2[ks, cs]))
            a[at, cs] = jnp.where(moved > 0, total, a[at, cs])

        loop(0, rb, step)
        for k in range(2):
            @pl.when(me == k)
            def _():
                half = np_ // 2
                a[pl.ds(0, nb), cs] = ag[pl.ds(k * half, half), pl.ds(0, ch), cs].reshape(nb, nb)

    def z_copy(i, zz, sem):
        at = panel.at[core, pl.ds(pl.multiple_of(i * piece, piece), piece), :]
        return pltpu.make_async_remote_copy(at, at, sem.at[i], z_recv.at[i], device_id=at_col(zz, core))

    def sib_copy(i):
        at = panel.at[core, pl.ds(pl.multiple_of(i * piece, piece), piece), :]
        return pltpu.make_async_remote_copy(at, at, sib_send.at[i], sib_recv.at[i], device_id=at_col(z, 1 - core))

    def sib_wait(i):
        at = panel.at[1 - core, pl.ds(pl.multiple_of(i * piece, piece), piece), :]
        pltpu.make_async_remote_copy(at, at, sib_send.at[i], sib_recv.at[i], device_id=at_col(z, 1 - core)).wait_recv()

    middle = nz // 2
    place(0)

    @pl.when(z == 0)
    def _():
        half = np_ // 2
        for k in range(2):
            @pl.when(core == k)
            def _():
                panel[core, pl.ds(0, nb), :] = ag[pl.ds((1 - k) * half, half), pl.ds(0, ch), pl.ds(0, nb)].reshape(nb, nb)
        panel[core, pl.ds(nb, rows), :] = a[:, pl.ds(0, nb)]

        def send(i):
            z_copy(i, 1, z_send).start()
            z_copy(i, nz - 1, z_send2).start()
            sib_copy(i).start()

        loop(0, CHUNKS, send)

    for c in range(1, cb):
        place(c)

    @pl.when(z != 0)
    def _():
        def relay(i):
            z_copy(i, z, z_send).wait_recv()

            @pl.when(jnp.logical_and(z < middle, z > 0))
            def _():
                z_copy(i, z + 1, z_send).start()

            @pl.when(z > middle + 1)
            def _():
                z_copy(i, z - 1, z_send).start()

            sib_copy(i).start()

        loop(0, CHUNKS, relay)

    ui0 = jnp.where(lane >= sub, inv[0], 0.0)
    ui1 = jnp.where(lane >= sub, inv[1], 0.0)
    eye = jnp.where(lane == sub, 1.0, 0.0)
    li0 = jnp.where(lane < sub, inv[0], 0.0) + eye
    li1 = jnp.where(lane < sub, inv[1], 0.0) + eye
    half = np_ // 2
    pr0 = ag[pl.ds(0, half), pl.ds(0, ch), :].reshape(nb, width)
    pr1 = ag[pl.ds(half, half), pl.ds(0, ch), :].reshape(nb, width)
    wide = lax.broadcasted_iota(jnp.int32, (nb, width), 1)
    block = jnp.where(wide < nb, col, 2 * nz)
    u0 = jnp.where(block > 0, product(li0, pr0), 0.0)

    loop(0, CHUNKS, sib_wait)
    l10 = product(panel[0, pl.ds(0, nb), :], ui0)
    u01 = product(li0, panel[1, pl.ds(0, nb), :])
    u1 = jnp.where(block > 1, product(li1, pr1 - product(l10, u0)), 0.0)
    u[pl.ds(0, nb), :], u[pl.ds(nb, nb), :] = u0, u1
    uh[pl.ds(0, nb), :], ul[pl.ds(0, nb), :] = parts2(u0)
    uh[pl.ds(nb, nb), :], ul[pl.ds(nb, nb), :] = parts2(u1)

    def store(r, c):
        return pltpu.make_async_copy(
            a.at[pl.ds(r * nb, nb), pl.ds(c * nb, nb)],
            out.at[r, 0, :, c, 0, :],
            out_sem.at[r * cb + c],
        )

    def update(r):
        at = pl.ds(pl.multiple_of(r * nb, nb), nb)
        below = pl.ds(pl.multiple_of(nb + r * nb, nb), nb)
        part = r * np_ + me
        l0 = jnp.where(part > 0, product(panel[0, below, :], ui0), 0.0)
        l1 = product(panel[1, below, :] - product(l0, u01), ui1)
        l1 = jnp.where(part > 1, l1, 0.0)
        total = a[at, :]
        for k, l in ((0, l0), (1, l1)):
            ks = pl.ds(k * nb, nb)
            h, m = parts2(l)
            total = total - (mul(h, uh[ks, :]) + (mul(h, ul[ks, :]) + mul(m, uh[ks, :])))
        new = jnp.where(jnp.logical_and(part == 0, block > 0), u[pl.ds(0, nb), :], total)
        new = jnp.where(jnp.logical_and(part == 1, block > 1), u[pl.ds(nb, nb), :], new)
        a[at, :] = new

        @pl.when(jnp.logical_and(col == 0, part > 0))
        def _():
            a[at, pl.ds(0, nb)] = l0

        @pl.when(jnp.logical_and(col == 1, part > 1))
        def _():
            a[at, pl.ds(0, nb)] = l1

    for r in range(rb):
        update(r)
        for c in range(cb):
            store(r, c).start()

    loop(1, np_, lambda d: rs_copy(d).wait_send())
    loop(1, np_, lambda d: ag_copy(d).wait_send())
    loop(0, CHUNKS, lambda i: sib_copy(i).wait_send())

    @pl.when(jnp.logical_or(z < middle, z > middle + 1))
    def _():
        loop(0, CHUNKS, lambda i: z_copy(i, z, z_send).wait_send())

    @pl.when(z == 0)
    def _():
        loop(0, CHUNKS, lambda i: z_copy(i, z, z_send2).wait_send())

    for r in range(rb):
        for c in range(cb):
            store(r, c).wait()


def shards(proc_rows, proc_cols, matrix, pivots, inverse_blocks):
    rb, _, nb, cb, _, _ = matrix.shape
    nz = proc_cols // 2
    rows, width, slots = rb * nb, cb * nb, 2 * nb
    ch, co = slots // proc_rows, nb // proc_rows
    dma = pltpu.SemaphoreType.DMA
    vmem = pl.BlockSpec(memory_space=pltpu.VMEM)
    return pl.pallas_call(
        functools.partial(kernel, (rb, cb, nb, proc_rows, nz)),
        out_shape=jax.ShapeDtypeStruct(matrix.shape, F32),
        in_specs=[pl.BlockSpec(memory_space=pl.ANY), vmem, vmem, vmem],
        out_specs=pl.BlockSpec(memory_space=pl.ANY),
        scratch_shapes=[
            pltpu.VMEM((rows, width), F32),
            pltpu.VMEM((rows, width), BF16),
            pltpu.VMEM((rows, width), BF16),
            pltpu.VMEM((rows, width), BF16),
            pltpu.VMEM((slots, width), F32),
            pltpu.VMEM((proc_rows, ch, width), F32),
            pltpu.VMEM((proc_rows, ch + 2 * co, width), F32),
            pltpu.VMEM((2, nb + rows, nb), F32),
            pltpu.VMEM((slots, width), F32),
            pltpu.VMEM((slots, width), BF16),
            pltpu.VMEM((slots, width), BF16),
            pltpu.VMEM((slots, width), BF16),
            pltpu.VMEM((slots, width), BF16),
            pltpu.VMEM((slots, width), BF16),
            dma((rb * cb,)), dma((rb * cb,)),
            dma((proc_rows,)), dma((proc_rows,)),
            dma((proc_rows,)), dma((2,)),
            dma((proc_rows,)), dma((proc_rows,)),
            dma((CHUNKS,)), dma((CHUNKS,)), dma((CHUNKS,)),
            dma((CHUNKS,)), dma((CHUNKS,)),
        ],
        compiler_params=pltpu.CompilerParams(
            collective_id=0, has_side_effects=True, vmem_limit_bytes=48 * 2**20
        ),
    )(matrix, pivots, pivots.T, inverse_blocks)


def solution(mesh):
    spec = P(None, "prow", None, None, "pcol", None)
    return jax.shard_map(
        functools.partial(shards, mesh.shape["prow"], mesh.shape["pcol"]),
        mesh=mesh,
        in_specs=(spec, P(), P()),
        out_specs=spec,
        check_vma=False,
    )
```

time: 960 us -> 121 us (0.13)
  the two profiles are of different devices: /device:TPU:32 before, /device:TPU:305 now
where the time goes in v1:
time: 121 us
  Pallas kernels  115 us (95%)
  local copies, waits for them, and re-layouts  5.44 us (4%)
    pallas_call x1, Pallas kernels, shards(): pl.pallas_call(functools.partial(kernel, (rb, cb, nb, proc_rows, nz)), ou...  115 us
    unnamed x8, local copies, waits for them, and re-layouts  5.44 us

profile of v1, /device:TPU:305, one launch (start us, length us, event | category | flops | bytes accessed | tf_op | source)
XLA Modules:
  0.0 120.9 jit_solution(11141722645461773374)
XLA Ops:
  0.0 0.8 copy.4
  0.8 0.0 copy-start
  0.8 1.6 %copy-done = f32[4,1,256,2,1,256]{5,4,3,2,1,0:T(1,128)S(1)} copy-done((f32[4,1,256,2,1,256]{5,4,3,2,1,0:T(1,128)S(1)}, f32[4,1,256,2,1,256]{5,4,3,2,1,0:T(1,128)}, u32[]{:S(2)}) %copy-start) | copy-done | bytes 2097176
  2.4 0.0 copy-start.1
  2.4 1.0 copy-done.1
  3.5 0.0 copy-start.2
  3.5 0.7 copy-done.2
  4.1 115.4 %shard_map.37 = f32[4,1,256,2,1,256]{5,4,3,2,1,0:T(1,128)S(1)} custom-call(f32[4,1,256,2,1,256]{5,4,3,2,1,0:T(1,128)S(1)} %copy-done, s32[2,256]{1,0:T(2,128)S(1)} %copy-done.2, s32[256,2]{1,0:T(8,128)S(1)} %bitcast.1, f32[2,256,256]{2,1,0:T(8,128)S(1)} %copy-done.1), custom_call_target="tpu_custom_call" | custom-call | tf_op jit(solution)/shard_map/pallas_call | solution.py:335
  119.6 1.3 %copy.6 = f32[4,1,256,2,1,256]{5,4,3,2,1,0:T(1,128)} copy(f32[4,1,256,2,1,256]{5,4,3,2,1,0:T(1,128)S(1)} %shard_map.37) | data formatting | bytes 4194304
Async XLA Ops:
  0.8 1.6 %copy-start = (f32[4,1,256,2,1,256]{5,4,3,2,1,0:T(1,128)S(1)}, f32[4,1,256,2,1,256]{5,4,3,2,1,0:T(1,128)}, u32[]{:S(2)}) copy-start(f32[4,1,256,2,1,256]{5,4,3,2,1,0:T(1,128)} %x.1) | copy-start | bytes 6291460
  2.4 1.0 copy-start.1
  3.5 0.7 copy-start.2

commit v2 on v0

v2 whole, which is shorter than its diff:
```python
import functools

import jax
import jax.numpy as jnp
from jax import lax
from jax.experimental import pallas as pl
from jax.experimental.pallas import tpu as pltpu
from jax.sharding import PartitionSpec as P

F32, BF16 = jnp.float32, jnp.bfloat16
PIECE_OF_BLOCK = 8
EXTRA = 11


def mul(left, right):
    return jnp.dot(left, right, preferred_element_type=F32)


def parts2(x):
    high = x.astype(BF16)
    return high, (x - high.astype(F32)).astype(BF16)


def parts3(x):
    high = x.astype(BF16)
    rest = x - high.astype(F32)
    mid = rest.astype(BF16)
    return high, mid, (rest - mid.astype(F32)).astype(BF16)


def across(*x):
    return jnp.concatenate(x, axis=1)


def down(*x):
    return jnp.concatenate(x, axis=0)


def weights(x):
    high, low = parts2(x)
    return down(high, low, high)


def product(left, right):
    high, low = parts2(left)
    return mul(across(high, high, low), weights(right))


def kernel(
    sizes, x, piv_in, inv_in, out,
    piv, inv, a, split, picks, rs, aold, apr, panel, corner, u, w0, w1, wu, old,
    in_sem, out_sem, rs_send, rs_recv, old_send, old_recv, aold_send, aold_recv, apr_send, apr_recv,
    z_send, z_send2, z_recv, sib_send, sib_recv,
):
    rb, cb, nb, np_, nz = sizes
    rows, slots = rb * nb, 2 * nb
    ch, co = slots // np_, nb // np_
    half = np_ // 2
    piece = nb // PIECE_OF_BLOCK
    chunks = (rb + 1) * PIECE_OF_BLOCK
    early = (rb - 1) * PIECE_OF_BLOCK
    me = lax.axis_index("prow")
    col = lax.axis_index("pcol")
    z, core = col // 2, col % 2
    middle = nz // 2

    def at_row(r):
        return {"prow": r, "pcol": col}

    def at_col(zz, cc):
        return {"prow": me, "pcol": zz * 2 + cc}

    def loop(low, high, body):
        def step(d, carry):
            body(d)
            return carry

        lax.fori_loop(low, high, step, 0)

    def load(r, c):
        return pltpu.make_async_copy(
            x.at[r, 0, :, c, 0, :], a.at[c, pl.ds(r * nb, nb), :], in_sem.at[r * cb + c]
        )

    load_piv = pltpu.make_async_copy(piv_in, piv, in_sem.at[rb * cb])
    load_inv = pltpu.make_async_copy(inv_in, inv, in_sem.at[rb * cb + 1])
    load_piv.start()
    for c in range(cb):
        for r in range(rb):
            load(r, c).start()
    load_inv.start()

    barrier = pltpu.get_barrier_semaphore()
    loop(1, np_, lambda d: pl.semaphore_signal(barrier, inc=1, device_id=at_row((me + d) % np_)))
    for zz, cc in (((z + 1) % nz, core), ((z + nz - 1) % nz, core), (z, 1 - core)):
        pl.semaphore_signal(barrier, inc=1, device_id=at_col(zz, cc))

    load_piv.wait()
    lane = lax.broadcasted_iota(jnp.int32, (nb, nb), 1)
    sub = lax.broadcasted_iota(jnp.int32, (nb, nb), 0)
    p0r, p1r = piv[0:1, :], piv[1:2, :]
    p0c = jnp.max(jnp.where(lane == sub, p0r, -1), axis=1, keepdims=True)
    p1c = jnp.max(jnp.where(lane == sub, p1r, -1), axis=1, keepdims=True)
    same = p1c == p0r
    back = jnp.max(jnp.where(same, lane, -1), axis=1, keepdims=True)
    src0, src1 = p0c, jnp.where(back >= 0, back, p1c)
    hit = jnp.max(jnp.where(p0r == sub + nb, p1c, -1), axis=0, keepdims=True)
    gone = jnp.max(jnp.where(same, 1, 0), axis=0, keepdims=True)
    dst0 = jnp.where(hit >= 0, hit, jnp.where(gone > 0, -1, p0r))
    up = jnp.max(jnp.where(p0c == lane + nb, 1, 0), axis=0, keepdims=True)
    dst1 = jnp.where(up > 0, -1, p1r)

    def old_copy(c, k, d):
        to = (me + d) % np_
        return pltpu.make_async_remote_copy(
            a.at[c, pl.ds(pl.multiple_of(to * co, co), co), :],
            aold.at[c, to, pl.ds(k * co, co), :],
            old_send.at[c], old_recv.at[c, k], device_id=at_row(to),
        )

    def old_scatter(c):
        for k in range(2):
            @pl.when(me == k)
            def _():
                loop(1, np_, lambda d: old_copy(c, k, d).start())
                aold[c, me, pl.ds(k * co, co), :] = a[c, pl.ds(pl.multiple_of(me * co, co), co), :]

    def old_ready(c):
        for k in range(2):
            @pl.when(me != k)
            def _():
                pltpu.make_async_remote_copy(
                    aold.at[c, me, pl.ds(k * co, co), :], aold.at[c, me, pl.ds(k * co, co), :],
                    old_send.at[c], old_recv.at[c, k], device_id=at_row((me + 1) % np_),
                ).wait_recv()

    def old_drain(c):
        for k in range(2):
            @pl.when(me == k)
            def _():
                sent = a.at[c, pl.ds(0, nb - co), :]
                pltpu.make_async_remote_copy(
                    sent, sent, old_send.at[c], old_recv.at[c, k], device_id=at_row((me + 1) % np_)
                ).wait_send()

    def gather(buf, send, recv, c):
        def start(d):
            pltpu.make_async_remote_copy(
                buf.at[c, me], buf.at[c, me], send.at[c], recv.at[c], device_id=at_row((me + d) % np_)
            ).start()

        loop(1, np_, start)

    def peers(buf, send, recv, c):
        others = buf.at[c, pl.ds(0, np_ - 1)]
        return pltpu.make_async_remote_copy(
            others, others, send.at[c], recv.at[c], device_id=at_row((me + 1) % np_)
        )

    def gather_wait(*which):
        peers(*which).wait_recv()

    old_g, pr_g = (aold, aold_send, aold_recv), (apr, apr_send, apr_recv)

    def pick(c):
        def step(r):
            h, m, l = parts3(a[c, pl.ds(pl.multiple_of(r * nb, nb), nb), :])
            split[0, pl.ds(pl.multiple_of(r * nb, nb), nb), :] = h
            split[1, pl.ds(pl.multiple_of(r * nb, nb), nb), :] = m
            split[2, pl.ds(pl.multiple_of(r * nb, nb), nb), :] = l

        loop(0, rb, step)
        for k, src in ((0, src0), (1, src1)):
            chosen = across(*[(src == (r * np_ + me) * nb + lane).astype(F32).astype(BF16) for r in range(rb)])
            picks[c, pl.ds(k * nb, nb), :] = mul(chosen, split[0]) + mul(chosen, split[1]) + mul(chosen, split[2])

    def rs_start(c):
        rs[c, me] = picks[c, pl.ds(pl.multiple_of(me * ch, ch), ch), :]

        def start(d):
            to = (me + d) % np_
            pltpu.make_async_remote_copy(
                picks.at[c, pl.ds(pl.multiple_of(to * ch, ch), ch), :], rs.at[c, me],
                rs_send.at[c], rs_recv.at[c], device_id=at_row(to),
            ).start()

        loop(1, np_, start)

    def rs_finish(c):
        peers(rs, rs_send, rs_recv, c).wait_recv()
        apr[c, me] = jnp.sum(rs[c], axis=0)

    def old_parts(c):
        for k in range(2):
            at = pl.ds(k * nb, nb)
            old[0, at, :], old[1, at, :], old[2, at, :] = parts3(aold[c, :, pl.ds(k * co, co), :].reshape(nb, nb))

    def place(c, r):
        at = pl.ds(r * nb, nb)
        here = (r * np_ + me) * nb + sub
        put0, put1 = (dst0 == here).astype(F32), (dst1 == here).astype(F32)
        moved = jnp.max(jnp.maximum(put0, put1), axis=1, keepdims=True)
        put = across(put0.astype(BF16), put1.astype(BF16))
        total = mul(put, old[0]) + mul(put, old[1]) + mul(put, old[2])
        a[c, at, :] = jnp.where(moved > 0, total, a[c, at, :])

    def piece_at(i, which):
        return panel.at[which, pl.ds(pl.multiple_of(i * piece, piece), piece), :]

    def z_copy(i, zz, sem):
        at = piece_at(i, core)
        return pltpu.make_async_remote_copy(at, at, sem, z_recv.at[i], device_id=at_col(zz, core))

    def sib_copy(i):
        at = piece_at(i, core)
        return pltpu.make_async_remote_copy(
            at, at, sib_send, sib_recv.at[i // PIECE_OF_BLOCK], device_id=at_col(z, 1 - core)
        )

    def sib_wait(t):
        at = panel.at[1 - core, pl.ds(t * nb, nb), :]
        pltpu.make_async_remote_copy(at, at, sib_send, sib_recv.at[t], device_id=at_col(z, 1 - core)).wait_recv()

    def send(i):
        z_copy(i, 1, z_send).start()
        z_copy(i, nz - 1, z_send2).start()
        sib_copy(i).start()

    def relay(i):
        z_copy(i, z, z_send).wait_recv()

        @pl.when(jnp.logical_and(z < middle, z > 0))
        def _():
            z_copy(i, z + 1, z_send).start()

        @pl.when(z > middle + 1)
        def _():
            z_copy(i, z - 1, z_send).start()

        sib_copy(i).start()

    def tile(r):
        return pl.ds((r if r < rb - 1 else rb) * nb, nb)

    solved = pl.ds((rb - 1) * nb, nb)

    def chosen_rows(c, k):
        return apr[c, pl.ds(k * half, half), :, :].reshape(nb, nb)

    def block(c):
        return col if c == 0 else c * 2 * nz + col

    def upper(k):
        return jnp.where(lane >= sub, inv[k], 0.0)

    def lower(k):
        return jnp.where(lane < sub, inv[k], 0.0) + jnp.where(lane == sub, 1.0, 0.0)

    def solve_first():
        w0[...] = weights(upper(0))
        for c in range(cb):
            u[c, pl.ds(0, nb), :] = jnp.where(block(c) > 0, product(lower(0), chosen_rows(c, 0)), 0.0)

    def solve_corner():
        sib_wait(rb - 1)
        corner[...] = product(panel[0, solved, :], upper(0))
        u01 = product(lower(0), panel[1, solved, :])
        cross = product(product(upper(0), u01), upper(1))
        w1[...] = weights(down(-cross, upper(1)))

    def solve_second():
        for c in range(cb):
            left = chosen_rows(c, 1) - product(corner[...], u[c, pl.ds(0, nb), :])
            u[c, pl.ds(nb, nb), :] = jnp.where(block(c) > 1, product(lower(1), left), 0.0)
            wu[:, pl.ds(c * nb, nb)] = weights(u[c])

    def store(r, c):
        return pltpu.make_async_copy(
            a.at[c, pl.ds(r * nb, nb), :], out.at[r, 0, :, c, 0, :], out_sem.at[r * cb + c]
        )

    def update(r):
        sib_wait(r if r < rb - 1 else rb)
        at = pl.ds(r * nb, nb)
        part = r * np_ + me
        c0h, c0l = parts2(panel[0, tile(r), :])
        c1h, c1l = parts2(panel[1, tile(r), :])
        l0 = mul(across(c0h, c0h, c0l), w0[...])
        l1 = mul(across(c0h, c1h, c0h, c1h, c0l, c1l), w1[...])
        if r == 0:
            l0 = jnp.where(me == 0, 0.0, jnp.where(me == 1, corner[...], l0))
            l1 = jnp.where(me <= 1, 0.0, l1)
        high, low = parts2(across(l0, l1))
        change = mul(across(high, high, low), wu[...])
        for c in range(cb):
            total = a[c, at, :]
            if r == 0:
                total = jnp.where(me == 0, chosen_rows(c, 0), jnp.where(me == 1, chosen_rows(c, 1), total))
            total = total - change[:, c * nb : (c + 1) * nb]
            if r == 0:
                for k in range(2):
                    mine = jnp.logical_and(part == k, block(c) > k)
                    total = jnp.where(mine, u[c, pl.ds(k * nb, nb), :], total)
            if c == 0:
                for k, l in enumerate((l0, l1)):
                    total = jnp.where(jnp.logical_and(col == k, part > k), l, total)
            a[c, at, :] = total
            store(r, c).start()

    load(0, 0).wait()
    pl.semaphore_wait(barrier, np_ - 1 + 3)
    old_scatter(0)
    for r in range(1, rb):
        load(r, 0).wait()
    pick(0)
    old_ready(0)
    gather(*old_g, 0)
    rs_start(0)
    for c in range(1, cb):
        for r in range(rb):
            load(r, c).wait()
        old_scatter(c)
    load_inv.wait()

    @pl.when(z == 0)
    def _():
        gather_wait(*old_g, 0)
        old_drain(0)
        old_parts(0)
        for r in range(rb):
            place(0, r)
            panel[core, tile(r), :] = a[0, pl.ds(r * nb, nb), :]
            if r < rb - 1:
                loop(r * PIECE_OF_BLOCK, (r + 1) * PIECE_OF_BLOCK, send)
        rs_finish(0)
        gather(*pr_g, 0)
        for c in range(1, cb):
            pick(c)
            old_ready(c)
        gather_wait(*pr_g, 0)
        for k in range(2):
            @pl.when(core == k)
            def _():
                panel[core, solved, :] = chosen_rows(0, 1 - k)
        loop(early, chunks, send)
        for c in range(1, cb):
            rs_start(c)
            gather(*old_g, c)
            rs_finish(c)
            gather(*pr_g, c)

    @pl.when(z != 0)
    def _():
        for c in range(1, cb):
            pick(c)
            rs_start(c)
            old_ready(c)
            gather(*old_g, c)

    def place_all(c):
        gather_wait(*old_g, c)
        old_drain(c)
        old_parts(c)
        for r in range(rb):
            place(c, r)

    def first_column():
        @pl.when(z != 0)
        def _():
            place_all(0)

    def second_column():
        for c in range(1, cb):
            place_all(c)

    def rows_here():
        @pl.when(z != 0)
        def _():
            gather_wait(*pr_g, 0)

        for c in range(1, cb):
            gather_wait(*pr_g, c)
        solve_first()

    def early_tiles():
        for r in range(rb - 1):
            update(r)

    near = jnp.where(z > middle, nz - z, z)
    turn = jnp.where(near < 5, 14 - 3 * near, 0)
    begin = 33 - 3 * near
    finish = jnp.where(near < middle - 1, chunks, early + PIECE_OF_BLOCK + 1)
    finish = jnp.where(begin + 15 > finish, begin + 15, finish)
    jobs = (
        (begin, first_column), (begin + 3, second_column), (begin + 14, rows_here),
        (finish, solve_corner), (finish + 1, solve_second), (finish + 2, early_tiles),
    )

    def step(i):
        @pl.when(jnp.logical_and(z != 0, i == turn))
        def _():
            for c in range(cb):
                rs_finish(c)
                gather(*pr_g, c)

        @pl.when(jnp.logical_and(z != 0, i < chunks))
        def _():
            relay(i)

        for when, job in jobs:
            pl.when(i == when)(job)

    loop(0, chunks + EXTRA, step)
    update(rb - 1)

    for c in range(cb):
        peers(rs, rs_send, rs_recv, c).wait_send()
        peers(*old_g, c).wait_send()
        peers(*pr_g, c).wait_send()
    whole = panel.at[core]

    def sent(sem):
        pltpu.make_async_remote_copy(whole, whole, sem, z_recv.at[0], device_id=at_col(z, 1 - core)).wait_send()

    sent(sib_send)

    @pl.when(jnp.logical_or(z < middle, z > middle + 1))
    def _():
        sent(z_send)

    @pl.when(z == 0)
    def _():
        sent(z_send2)

    for r in range(rb):
        for c in range(cb):
            store(r, c).wait()


def shards(proc_rows, proc_cols, matrix, pivots, inverse_blocks):
    rb, _, nb, cb, _, _ = matrix.shape
    nz = proc_cols // 2
    rows, slots = rb * nb, 2 * nb
    ch, co = slots // proc_rows, nb // proc_rows
    chunks = (rb + 1) * PIECE_OF_BLOCK
    dma = pltpu.SemaphoreType.DMA
    far = pl.BlockSpec(memory_space=pltpu.HBM)
    pair = dma((cb,))
    return pl.pallas_call(
        functools.partial(kernel, (rb, cb, nb, proc_rows, nz)),
        out_shape=jax.ShapeDtypeStruct(matrix.shape, F32),
        in_specs=[far, far, far],
        out_specs=pl.BlockSpec(memory_space=pl.ANY),
        scratch_shapes=[
            pltpu.VMEM(pivots.shape, jnp.int32),
            pltpu.VMEM(inverse_blocks.shape, F32),
            pltpu.VMEM((cb, rows, nb), F32),
            pltpu.VMEM((3, rows, nb), BF16),
            pltpu.VMEM((cb, slots, nb), F32),
            pltpu.VMEM((cb, proc_rows, ch, nb), F32),
            pltpu.VMEM((cb, proc_rows, 2 * co, nb), F32),
            pltpu.VMEM((cb, proc_rows, ch, nb), F32),
            pltpu.VMEM((2, rows + nb, nb), F32),
            pltpu.VMEM((nb, nb), F32),
            pltpu.VMEM((cb, slots, nb), F32),
            pltpu.VMEM((3 * nb, nb), BF16),
            pltpu.VMEM((6 * nb, nb), BF16),
            pltpu.VMEM((6 * nb, cb * nb), BF16),
            pltpu.VMEM((3, slots, nb), BF16),
            dma((rb * cb + 2,)), dma((rb * cb,)),
            pair, pair, pair, dma((cb, 2)), pair, pair, pair, pair,
            dma, dma, dma((chunks,)), dma, dma((rb + 1,)),
        ],
        compiler_params=pltpu.CompilerParams(
            collective_id=0, has_side_effects=True, vmem_limit_bytes=50 * 2**20
        ),
    )(matrix, pivots, inverse_blocks)


def solution(mesh):
    spec = P(None, "prow", None, None, "pcol", None)
    return jax.shard_map(
        functools.partial(shards, mesh.shape["prow"], mesh.shape["pcol"]),
        mesh=mesh,
        in_specs=(spec, P(), P()),
        out_specs=spec,
        check_vma=False,
    )
```

time: 960 us -> 83.3 us (0.09)
  the two profiles are of different devices: /device:TPU:32 before, /device:TPU:305 now
where the time goes in v2:
time: 83.3 us; the launch traced here: 83.1 us
  Pallas kernels  80.1 us (96%)
  local copies, waits for them, and re-layouts  3.04 us (4%)
    pallas_call x1, Pallas kernels, shards(): pl.pallas_call(functools.partial(kernel, (rb, cb, nb, proc_rows, nz)), ou...  80.1 us
    unnamed x5, local copies, waits for them, and re-layouts  3.04 us

profile of v2, /device:TPU:305, one launch (start us, length us, event | category | flops | bytes accessed | tf_op | source)
XLA Modules:
  0.0 83.1 jit_solution(9565765168166389859)
XLA Ops:
  0.0 0.0 copy-start
  0.0 1.0 %copy-done = f32[2,256,256]{2,1,0:T(8,128)S(1)} copy-done((f32[2,256,256]{2,1,0:T(8,128)S(1)}, f32[2,256,256]{2,1,0:T(8,128)}, u32[]{:S(2)}) %copy-start) | copy-done | bytes 524312
  1.0 0.0 copy-start.1
  1.0 0.7 copy-done.1
  1.7 80.1 %shard_map.37 = f32[4,1,256,2,1,256]{5,4,3,2,1,0:T(1,128)S(1)} custom-call(f32[4,1,256,2,1,256]{5,4,3,2,1,0:T(1,128)} %x.1, s32[2,256]{1,0:T(2,128)S(1)} %copy-done.1, f32[2,256,256]{2,1,0:T(8,128)S(1)} %copy-done), custom_call_target="tpu_custom_call" | custom-call | tf_op jit(solution)/shard_map/pallas_call | solution.py:449
  81.8 1.3 %copy.5 = f32[4,1,256,2,1,256]{5,4,3,2,1,0:T(1,128)} copy(f32[4,1,256,2,1,256]{5,4,3,2,1,0:T(1,128)S(1)} %shard_map.37) | data formatting | bytes 4194304
Async XLA Ops:
  0.0 1.0 %copy-start = (f32[2,256,256]{2,1,0:T(8,128)S(1)}, f32[2,256,256]{2,1,0:T(8,128)}, u32[]{:S(2)}) copy-start(f32[2,256,256]{2,1,0:T(8,128)} %inv_in.1) | copy-start | bytes 1572868
  1.0 0.7 copy-start.1

commit v3 on v2

--- a/solution.py
+++ b/solution.py
@@ -9,7 +9,7 @@
 
 F32, BF16 = jnp.float32, jnp.bfloat16
 PIECE_OF_BLOCK = 8
-EXTRA = 11
+OLD_AT, ROWS_AT = 4, 18
 
 
 def mul(left, right):
@@ -48,17 +48,16 @@
 
 def kernel(
     sizes, x, piv_in, inv_in, out,
-    piv, inv, a, split, picks, rs, aold, apr, panel, corner, u, w0, w1, wu, old,
+    piv, inv, a, split, picks, rs, aold, apr, panel, cor, l10, u, w0, w1, wu, old, cold,
     in_sem, out_sem, rs_send, rs_recv, old_send, old_recv, aold_send, aold_recv, apr_send, apr_recv,
-    z_send, z_send2, z_recv, sib_send, sib_recv,
+    z_send, z_send2, zc_send, zc_send2, z_recv, sib_send, sib_recv, cor_send, cor_recv, sibc_send, sibc_recv,
 ):
     rb, cb, nb, np_, nz = sizes
     rows, slots = rb * nb, 2 * nb
     ch, co = slots // np_, nb // np_
     half = np_ // 2
     piece = nb // PIECE_OF_BLOCK
-    chunks = (rb + 1) * PIECE_OF_BLOCK
-    early = (rb - 1) * PIECE_OF_BLOCK
+    chunks = rb * PIECE_OF_BLOCK
     me = lax.axis_index("prow")
     col = lax.axis_index("pcol")
     z, core = col // 2, col % 2
@@ -195,21 +194,41 @@
             at = pl.ds(k * nb, nb)
             old[0, at, :], old[1, at, :], old[2, at, :] = parts3(aold[c, :, pl.ds(k * co, co), :].reshape(nb, nb))
 
+    def moves(r):
+        here = (r * np_ + me) * nb + sub
+        put0, put1 = (dst0 == here).astype(F32), (dst1 == here).astype(F32)
+        moved = jnp.max(jnp.maximum(put0, put1), axis=1, keepdims=True) > 0
+        return across(put0.astype(BF16), put1.astype(BF16)), moved
+
     def place(c, r):
         at = pl.ds(r * nb, nb)
-        here = (r * np_ + me) * nb + sub
-        put0, put1 = (dst0 == here).astype(F32), (dst1 == here).astype(F32)
-        moved = jnp.max(jnp.maximum(put0, put1), axis=1, keepdims=True)
-        put = across(put0.astype(BF16), put1.astype(BF16))
+        put, moved = moves(r)
         total = mul(put, old[0]) + mul(put, old[1]) + mul(put, old[2])
-        a[c, at, :] = jnp.where(moved > 0, total, a[c, at, :])
+        a[c, at, :] = jnp.where(moved, total, a[c, at, :])
 
     def piece_at(i, which):
         return panel.at[which, pl.ds(pl.multiple_of(i * piece, piece), piece), :]
 
-    def z_copy(i, zz, sem):
-        at = piece_at(i, core)
-        return pltpu.make_async_remote_copy(at, at, sem, z_recv.at[i], device_id=at_col(zz, core))
+    def corner_at(j):
+        return cor.at[core, me, pl.ds(j * ch, ch), :]
+
+    def z_copy(at, k, zz, sem):
+        return pltpu.make_async_remote_copy(at, at, sem, z_recv.at[k], device_id=at_col(zz, core))
+
+    def z_both(at, k, plus, minus):
+        z_copy(at, k, 1, plus).start()
+        z_copy(at, k, nz - 1, minus).start()
+
+    def z_on(at, k, sem):
+        z_copy(at, k, z, sem).wait_recv()
+
+        @pl.when(jnp.logical_and(z < middle, z > 0))
+        def _():
+            z_copy(at, k, z + 1, sem).start()
+
+        @pl.when(z > middle + 1)
+        def _():
+            z_copy(at, k, z - 1, sem).start()
 
     def sib_copy(i):
         at = piece_at(i, core)
@@ -221,28 +240,19 @@
         at = panel.at[1 - core, pl.ds(t * nb, nb), :]
         pltpu.make_async_remote_copy(at, at, sib_send, sib_recv.at[t], device_id=at_col(z, 1 - core)).wait_recv()
 
+    def cor_copy(which):
+        at = cor.at[which]
+        return pltpu.make_async_remote_copy(at, at, sibc_send, sibc_recv, device_id=at_col(z, 1 - core))
+
+    cor_g = cor, cor_send, cor_recv, core
+
     def send(i):
-        z_copy(i, 1, z_send).start()
-        z_copy(i, nz - 1, z_send2).start()
+        z_both(piece_at(i, core), i, z_send, z_send2)
         sib_copy(i).start()
 
     def relay(i):
-        z_copy(i, z, z_send).wait_recv()
-
-        @pl.when(jnp.logical_and(z < middle, z > 0))
-        def _():
-            z_copy(i, z + 1, z_send).start()
-
-        @pl.when(z > middle + 1)
-        def _():
-            z_copy(i, z - 1, z_send).start()
-
+        z_on(piece_at(i, core), i, z_send)
         sib_copy(i).start()
-
-    def tile(r):
-        return pl.ds((r if r < rb - 1 else rb) * nb, nb)
-
-    solved = pl.ds((rb - 1) * nb, nb)
 
     def chosen_rows(c, k):
         return apr[c, pl.ds(k * half, half), :, :].reshape(nb, nb)
@@ -262,15 +272,21 @@
             u[c, pl.ds(0, nb), :] = jnp.where(block(c) > 0, product(lower(0), chosen_rows(c, 0)), 0.0)
 
     def solve_corner():
-        sib_wait(rb - 1)
-        corner[...] = product(panel[0, solved, :], upper(0))
-        u01 = product(lower(0), panel[1, solved, :])
+        first = cor[0, pl.ds(half, half), pl.ds(ch, ch), :].reshape(nb, nb)
+        second = cor[1, pl.ds(0, half), pl.ds(ch, ch), :].reshape(nb, nb)
+        l10[...] = product(first, upper(0))
+        u01 = product(lower(0), second)
         cross = product(product(upper(0), u01), upper(1))
         w1[...] = weights(down(-cross, upper(1)))
+        for b in range(2):
+            for k in range(2):
+                high, low = parts2(cor[b, :, pl.ds(k * co, co), :].reshape(nb, nb))
+                cold[0, pl.ds(k * nb, nb), pl.ds(b * nb, nb)] = high
+                cold[1, pl.ds(k * nb, nb), pl.ds(b * nb, nb)] = low
 
     def solve_second():
         for c in range(cb):
-            left = chosen_rows(c, 1) - product(corner[...], u[c, pl.ds(0, nb), :])
+            left = chosen_rows(c, 1) - product(l10[...], u[c, pl.ds(0, nb), :])
             u[c, pl.ds(nb, nb), :] = jnp.where(block(c) > 1, product(lower(1), left), 0.0)
             wu[:, pl.ds(c * nb, nb)] = weights(u[c])
 
@@ -280,15 +296,16 @@
         )
 
     def update(r):
-        sib_wait(r if r < rb - 1 else rb)
+        sib_wait(r)
         at = pl.ds(r * nb, nb)
         part = r * np_ + me
-        c0h, c0l = parts2(panel[0, tile(r), :])
-        c1h, c1l = parts2(panel[1, tile(r), :])
-        l0 = mul(across(c0h, c0h, c0l), w0[...])
-        l1 = mul(across(c0h, c1h, c0h, c1h, c0l, c1l), w1[...])
+        put, moved = moves(r)
+        both = jnp.where(moved, mul(put, cold[0]) + mul(put, cold[1]), across(panel[0, at, :], panel[1, at, :]))
+        high, low = parts2(both)
+        l0 = mul(across(high[:, :nb], high[:, :nb], low[:, :nb]), w0[...])
+        l1 = mul(across(high, high, low), w1[...])
         if r == 0:
-            l0 = jnp.where(me == 0, 0.0, jnp.where(me == 1, corner[...], l0))
+            l0 = jnp.where(me == 0, 0.0, jnp.where(me == 1, l10[...], l0))
             l1 = jnp.where(me <= 1, 0.0, l1)
         high, low = parts2(across(l0, l1))
         change = mul(across(high, high, low), wu[...])
@@ -312,125 +329,111 @@
     old_scatter(0)
     for r in range(1, rb):
         load(r, 0).wait()
+
+    @pl.when(z == 0)
+    def _():
+        panel[core] = a[0]
+        loop(0, OLD_AT, send)
+
     pick(0)
+    rs_start(0)
     old_ready(0)
+
+    @pl.when(z == 0)
+    def _():
+        cor[core, me, pl.ds(0, ch), :] = aold[0, me]
+        z_both(corner_at(0), chunks, zc_send, zc_send2)
+        loop(OLD_AT, ROWS_AT, send)
+
     gather(*old_g, 0)
-    rs_start(0)
     for c in range(1, cb):
         for r in range(rb):
             load(r, c).wait()
         old_scatter(c)
+        pick(c)
+        rs_start(c)
+        old_ready(c)
+        gather(*old_g, c)
     load_inv.wait()
 
+    def chosen_ready():
+        for c in range(cb):
+            rs_finish(c)
+            gather(*pr_g, c)
+
     @pl.when(z == 0)
     def _():
-        gather_wait(*old_g, 0)
-        old_drain(0)
-        old_parts(0)
-        for r in range(rb):
-            place(0, r)
-            panel[core, tile(r), :] = a[0, pl.ds(r * nb, nb), :]
-            if r < rb - 1:
-                loop(r * PIECE_OF_BLOCK, (r + 1) * PIECE_OF_BLOCK, send)
         rs_finish(0)
+        cor[core, me, pl.ds(ch, ch), :] = apr[0, me]
+        z_both(corner_at(1), chunks + 1, zc_send, zc_send2)
+        loop(ROWS_AT, chunks, send)
+        gather(*cor_g)
         gather(*pr_g, 0)
         for c in range(1, cb):
-            pick(c)
-            old_ready(c)
-        gather_wait(*pr_g, 0)
-        for k in range(2):
-            @pl.when(core == k)
-            def _():
-                panel[core, solved, :] = chosen_rows(0, 1 - k)
-        loop(early, chunks, send)
-        for c in range(1, cb):
-            rs_start(c)
-            gather(*old_g, c)
             rs_finish(c)
             gather(*pr_g, c)
 
     @pl.when(z != 0)
     def _():
-        for c in range(1, cb):
-            pick(c)
-            rs_start(c)
-            old_ready(c)
-            gather(*old_g, c)
-
-    def place_all(c):
+        near = jnp.where(z > middle, nz - z, z)
+        turn = 28 - 3 * near
+
+        def step(i):
+            @pl.when(i == turn)
+            def _():
+                chosen_ready()
+
+            @pl.when(i == OLD_AT)
+            def _():
+                z_on(corner_at(0), chunks, zc_send)
+
+            @pl.when(i == ROWS_AT)
+            def _():
+                z_on(corner_at(1), chunks + 1, zc_send)
+                gather(*cor_g)
+
+            relay(i)
+
+        loop(0, chunks, step)
+
+    for c in range(cb):
         gather_wait(*old_g, c)
         old_drain(c)
         old_parts(c)
         for r in range(rb):
             place(c, r)
-
-    def first_column():
-        @pl.when(z != 0)
-        def _():
-            place_all(0)
-
-    def second_column():
-        for c in range(1, cb):
-            place_all(c)
-
-    def rows_here():
-        @pl.when(z != 0)
-        def _():
-            gather_wait(*pr_g, 0)
-
-        for c in range(1, cb):
-            gather_wait(*pr_g, c)
-        solve_first()
-
-    def early_tiles():
-        for r in range(rb - 1):
-            update(r)
-
-    near = jnp.where(z > middle, nz - z, z)
-    turn = jnp.where(near < 5, 14 - 3 * near, 0)
-    begin = 33 - 3 * near
-    finish = jnp.where(near < middle - 1, chunks, early + PIECE_OF_BLOCK + 1)
-    finish = jnp.where(begin + 15 > finish, begin + 15, finish)
-    jobs = (
-        (begin, first_column), (begin + 3, second_column), (begin + 14, rows_here),
-        (finish, solve_corner), (finish + 1, solve_second), (finish + 2, early_tiles),
-    )
-
-    def step(i):
-        @pl.when(jnp.logical_and(z != 0, i == turn))
-        def _():
-            for c in range(cb):
-                rs_finish(c)
-                gather(*pr_g, c)
-
-        @pl.when(jnp.logical_and(z != 0, i < chunks))
-        def _():
-            relay(i)
-
-        for when, job in jobs:
-            pl.when(i == when)(job)
-
-    loop(0, chunks + EXTRA, step)
-    update(rb - 1)
+    gather_wait(*cor_g)
+    cor_copy(core).start()
+    for c in range(cb):
+        gather_wait(*pr_g, c)
+    solve_first()
+    cor_copy(1 - core).wait_recv()
+    solve_corner()
+    solve_second()
+    for r in range(rb):
+        update(r)
 
     for c in range(cb):
         peers(rs, rs_send, rs_recv, c).wait_send()
         peers(*old_g, c).wait_send()
         peers(*pr_g, c).wait_send()
-    whole = panel.at[core]
-
-    def sent(sem):
-        pltpu.make_async_remote_copy(whole, whole, sem, z_recv.at[0], device_id=at_col(z, 1 - core)).wait_send()
-
-    sent(sib_send)
+    peers(*cor_g).wait_send()
+    cor_copy(core).wait_send()
+
+    def sent(at, sem):
+        z_copy(at, 0, z, sem).wait_send()
+
+    sent(panel.at[core], sib_send)
 
     @pl.when(jnp.logical_or(z < middle, z > middle + 1))
     def _():
-        sent(z_send)
+        sent(panel.at[core], z_send)
+        sent(cor.at[core, me], zc_send)
 
     @pl.when(z == 0)
     def _():
-        sent(z_send2)
+        sent(panel.at[core], z_send2)
+        sent(cor.at[core, me], zc_send2)
 
     for r in range(rb):
         for c in range(cb):
@@ -442,7 +445,7 @@
     nz = proc_cols // 2
     rows, slots = rb * nb, 2 * nb
     ch, co = slots // proc_rows, nb // proc_rows
-    chunks = (rb + 1) * PIECE_OF_BLOCK
+    chunks = rb * PIECE_OF_BLOCK
     dma = pltpu.SemaphoreType.DMA
     far = pl.BlockSpec(memory_space=pltpu.HBM)
     pair = dma((cb,))
@@ -460,16 +463,18 @@
             pltpu.VMEM((cb, proc_rows, ch, nb), F32),
             pltpu.VMEM((cb, proc_rows, 2 * co, nb), F32),
             pltpu.VMEM((cb, proc_rows, ch, nb), F32),
-            pltpu.VMEM((2, rows + nb, nb), F32),
+            pltpu.VMEM((2, rows, nb), F32),
+            pltpu.VMEM((2, proc_rows, 2 * ch, nb), F32),
             pltpu.VMEM((nb, nb), F32),
             pltpu.VMEM((cb, slots, nb), F32),
             pltpu.VMEM((3 * nb, nb), BF16),
             pltpu.VMEM((6 * nb, nb), BF16),
             pltpu.VMEM((6 * nb, cb * nb), BF16),
             pltpu.VMEM((3, slots, nb), BF16),
+            pltpu.VMEM((2, slots, 2 * nb), BF16),
             dma((rb * cb + 2,)), dma((rb * cb,)),
             pair, pair, pair, dma((cb, 2)), pair, pair, pair, pair,
-            dma, dma, dma((chunks,)), dma, dma((rb + 1,)),
+            dma, dma, dma, dma, dma((chunks + 2,)), dma, dma((rb,)), dma((2,)), dma((2,)), dma, dma,
         ],
         compiler_params=pltpu.CompilerParams(
             collective_id=0, has_side_effects=True, vmem_limit_bytes=50 * 2**20

time: 83.3 us -> 86.1 us (1.034)
  the two profiles are of different devices: /device:TPU:305 before, /device:TPU:297 now
where the time goes in v3:
time: 86.1 us; the launch traced here: 85.9 us
  Pallas kernels  82.8 us (96%)
  local copies, waits for them, and re-layouts  3.04 us (4%)
    pallas_call x1, Pallas kernels, shards(): pl.pallas_call(functools.partial(kernel, (rb, cb, nb, proc_rows, nz)), ou...  82.8 us
    unnamed x5, local copies, waits for them, and re-layouts  3.04 us

profile of v3, /device:TPU:297, one launch (start us, length us, event | category | flops | bytes accessed | tf_op | source)
XLA Modules:
  0.0 85.9 jit_solution(3778576574082703109)
XLA Ops:
  0.0 0.0 copy-start
  0.0 1.0 %copy-done = f32[2,256,256]{2,1,0:T(8,128)S(1)} copy-done((f32[2,256,256]{2,1,0:T(8,128)S(1)}, f32[2,256,256]{2,1,0:T(8,128)}, u32[]{:S(2)}) %copy-start) | copy-done | bytes 524312
  1.0 0.0 copy-start.1
  1.0 0.7 copy-done.1
  1.7 82.8 %shard_map.37 = f32[4,1,256,2,1,256]{5,4,3,2,1,0:T(1,128)S(1)} custom-call(f32[4,1,256,2,1,256]{5,4,3,2,1,0:T(1,128)} %x.1, s32[2,256]{1,0:T(2,128)S(1)} %copy-done.1, f32[2,256,256]{2,1,0:T(8,128)S(1)} %copy-done), custom_call_target="tpu_custom_call" | custom-call | tf_op jit(solution)/shard_map/pallas_call | solution.py:452
  84.5 1.3 %copy.5 = f32[4,1,256,2,1,256]{5,4,3,2,1,0:T(1,128)} copy(f32[4,1,256,2,1,256]{5,4,3,2,1,0:T(1,128)S(1)} %shard_map.37) | data formatting | bytes 4194304
Async XLA Ops:
  0.0 1.0 %copy-start = (f32[2,256,256]{2,1,0:T(8,128)S(1)}, f32[2,256,256]{2,1,0:T(8,128)}, u32[]{:S(2)}) copy-start(f32[2,256,256]{2,1,0:T(8,128)} %inv_in.1) | copy-start | bytes 1572868
  1.0 0.7 copy-start.1

commit v4 on v3

--- a/solution.py
+++ b/solution.py
@@ -9,7 +9,7 @@
 
 F32, BF16 = jnp.float32, jnp.bfloat16
 PIECE_OF_BLOCK = 8
-OLD_AT, ROWS_AT = 4, 18
+OLD_AT, ROWS_AT, PLACE_AT = 4, 18, 24
 
 
 def mul(left, right):
@@ -91,8 +91,23 @@
 
     barrier = pltpu.get_barrier_semaphore()
     loop(1, np_, lambda d: pl.semaphore_signal(barrier, inc=1, device_id=at_row((me + d) % np_)))
-    for zz, cc in (((z + 1) % nz, core), ((z + nz - 1) % nz, core), (z, 1 - core)):
-        pl.semaphore_signal(barrier, inc=1, device_id=at_col(zz, cc))
+    pl.semaphore_signal(barrier, inc=1, device_id=at_col(z, 1 - core))
+
+    @pl.when(z == 0)
+    def _():
+        loop(1, nz, lambda zz: pl.semaphore_signal(barrier, inc=1, device_id=at_col(zz, core)))
+
+    @pl.when(z != 0)
+    def _():
+        pl.semaphore_signal(barrier, inc=1, device_id=at_col(0, core))
+
+    @pl.when(z > 1)
+    def _():
+        pl.semaphore_signal(barrier, inc=1, device_id=at_col(z - 1, core))
+
+    @pl.when(jnp.logical_and(z > 0, z < nz - 1))
+    def _():
+        pl.semaphore_signal(barrier, inc=1, device_id=at_col(z + 1, core))
 
     load_piv.wait()
     lane = lax.broadcasted_iota(jnp.int32, (nb, nb), 1)
@@ -325,7 +340,18 @@
             store(r, c).start()
 
     load(0, 0).wait()
-    pl.semaphore_wait(barrier, np_ - 1 + 3)
+    @pl.when(z == 0)
+    def _():
+        pl.semaphore_wait(barrier, np_ + nz - 1)
+
+    @pl.when(jnp.logical_or(z == 1, z == nz - 1))
+    def _():
+        pl.semaphore_wait(barrier, np_ + 2)
+
+    @pl.when(jnp.logical_and(z > 1, z < nz - 1))
+    def _():
+        pl.semaphore_wait(barrier, np_ + 3)
+
     old_scatter(0)
     for r in range(1, rb):
         load(r, 0).wait()
@@ -342,7 +368,7 @@
     @pl.when(z == 0)
     def _():
         cor[core, me, pl.ds(0, ch), :] = aold[0, me]
-        z_both(corner_at(0), chunks, zc_send, zc_send2)
+        z_both(corner_at(0), chunks, zc_send, zc_send2.at[0])
         loop(OLD_AT, ROWS_AT, send)
 
     gather(*old_g, 0)
@@ -356,8 +382,23 @@
         gather(*old_g, c)
     load_inv.wait()
 
-    def chosen_ready():
+    def corner_to(zz):
+        return z_copy(corner_at(1), chunks + 1, zz, zc_send2.at[zz])
+
+    def place_all():
         for c in range(cb):
+            gather_wait(*old_g, c)
+            old_drain(c)
+            old_parts(c)
+            for r in range(rb):
+                place(c, r)
+
+    def first_ready():
+        rs_finish(0)
+        gather(*pr_g, 0)
+
+    def others_ready():
+        for c in range(1, cb):
             rs_finish(c)
             gather(*pr_g, c)
 
@@ -365,43 +406,36 @@
     def _():
         rs_finish(0)
         cor[core, me, pl.ds(ch, ch), :] = apr[0, me]
-        z_both(corner_at(1), chunks + 1, zc_send, zc_send2)
+        loop(1, nz, lambda zz: corner_to(zz).start())
         loop(ROWS_AT, chunks, send)
         gather(*cor_g)
         gather(*pr_g, 0)
-        for c in range(1, cb):
-            rs_finish(c)
-            gather(*pr_g, c)
+        others_ready()
+        place_all()
 
     @pl.when(z != 0)
     def _():
         near = jnp.where(z > middle, nz - z, z)
-        turn = 28 - 3 * near
+        turn = jnp.where(near < 2, PLACE_AT - 1, 28 - 3 * near)
 
         def step(i):
-            @pl.when(i == turn)
-            def _():
-                chosen_ready()
-
             @pl.when(i == OLD_AT)
             def _():
                 z_on(corner_at(0), chunks, zc_send)
 
-            @pl.when(i == ROWS_AT)
+            @pl.when(i == turn)
             def _():
-                z_on(corner_at(1), chunks + 1, zc_send)
+                first_ready()
+                corner_to(z).wait_recv()
                 gather(*cor_g)
+                others_ready()
 
             relay(i)
 
-        loop(0, chunks, step)
-
-    for c in range(cb):
-        gather_wait(*old_g, c)
-        old_drain(c)
-        old_parts(c)
-        for r in range(rb):
-            place(c, r)
+        loop(0, PLACE_AT, step)
+        place_all()
+        loop(PLACE_AT, chunks, step)
+
     gather_wait(*cor_g)
     cor_copy(core).start()
     for c in range(cb):
@@ -428,12 +462,13 @@
     @pl.when(jnp.logical_or(z < middle, z > middle + 1))
     def _():
         sent(panel.at[core], z_send)
-        sent(cor.at[core, me], zc_send)
+        sent(corner_at(0), zc_send)
 
     @pl.when(z == 0)
     def _():
         sent(panel.at[core], z_send2)
-        sent(cor.at[core, me], zc_send2)
+        sent(corner_at(0), zc_send2.at[0])
+        loop(1, nz, lambda zz: corner_to(zz).wait_send())
 
     for r in range(rb):
         for c in range(cb):
@@ -474,7 +509,7 @@
             pltpu.VMEM((2, slots, 2 * nb), BF16),
             dma((rb * cb + 2,)), dma((rb * cb,)),
             pair, pair, pair, dma((cb, 2)), pair, pair, pair, pair,
-            dma, dma, dma, dma, dma((chunks + 2,)), dma, dma((rb,)), dma((2,)), dma((2,)), dma, dma,
+            dma, dma, dma, dma((nz,)), dma((chunks + 2,)), dma, dma((rb,)), dma((2,)), dma((2,)), dma, dma,
         ],
         compiler_params=pltpu.CompilerParams(
             collective_id=0, has_side_effects=True, vmem_limit_bytes=50 * 2**20

time: 86.1 us -> 87.4 us (1.015)
  the two profiles are of different devices: /device:TPU:297 before, /device:TPU:355 now
where the time goes in v4:
time: 87.4 us; the launch traced here: 87.2 us
  Pallas kernels  84.1 us (96%)
  local copies, waits for them, and re-layouts  3.04 us (3%)
    pallas_call x1, Pallas kernels, shards(): pl.pallas_call(functools.partial(kernel, (rb, cb, nb, proc_rows, nz)), ou...  84.1 us
    unnamed x5, local copies, waits for them, and re-layouts  3.04 us

profile of v4, /device:TPU:355, one launch (start us, length us, event | category | flops | bytes accessed | tf_op | source)
XLA Modules:
  0.0 87.2 jit_solution(2839466648783863877)
XLA Ops:
  0.0 0.0 copy-start
  0.0 1.0 %copy-done = f32[2,256,256]{2,1,0:T(8,128)S(1)} copy-done((f32[2,256,256]{2,1,0:T(8,128)S(1)}, f32[2,256,256]{2,1,0:T(8,128)}, u32[]{:S(2)}) %copy-start) | copy-done | bytes 524312
  1.0 0.0 copy-start.1
  1.0 0.7 copy-done.1
  1.7 84.1 %shard_map.37 = f32[4,1,256,2,1,256]{5,4,3,2,1,0:T(1,128)S(1)} custom-call(f32[4,1,256,2,1,256]{5,4,3,2,1,0:T(1,128)} %x.1, s32[2,256]{1,0:T(2,128)S(1)} %copy-done.1, f32[2,256,256]{2,1,0:T(8,128)S(1)} %copy-done), custom_call_target="tpu_custom_call" | custom-call | tf_op jit(solution)/shard_map/pallas_call | solution.py:487
  85.9 1.3 %copy.5 = f32[4,1,256,2,1,256]{5,4,3,2,1,0:T(1,128)} copy(f32[4,1,256,2,1,256]{5,4,3,2,1,0:T(1,128)S(1)} %shard_map.37) | data formatting | bytes 4194304
Async XLA Ops:
  0.0 1.0 %copy-start = (f32[2,256,256]{2,1,0:T(8,128)S(1)}, f32[2,256,256]{2,1,0:T(8,128)}, u32[]{:S(2)}) copy-start(f32[2,256,256]{2,1,0:T(8,128)} %inv_in.1) | copy-start | bytes 1572868
  1.0 0.7 copy-start.1

commit v5 on v2

--- a/solution.py
+++ b/solution.py
@@ -357,21 +357,15 @@
             old_ready(c)
             gather(*old_g, c)
 
-    def place_all(c):
+    def old_here(c):
         gather_wait(*old_g, c)
         old_drain(c)
         old_parts(c)
-        for r in range(rb):
-            place(c, r)
-
-    def first_column():
+
+    def unless_first(body, *args):
         @pl.when(z != 0)
         def _():
-            place_all(0)
-
-    def second_column():
-        for c in range(1, cb):
-            place_all(c)
+            body(*args)
 
     def rows_here():
         @pl.when(z != 0)
@@ -389,12 +383,15 @@
     near = jnp.where(z > middle, nz - z, z)
     turn = jnp.where(near < 5, 14 - 3 * near, 0)
     begin = 33 - 3 * near
-    finish = jnp.where(near < middle - 1, chunks, early + PIECE_OF_BLOCK + 1)
+    last = jnp.logical_or(z == middle, z == middle + 1)
+    finish = jnp.where(last, early + PIECE_OF_BLOCK + 1, chunks)
     finish = jnp.where(begin + 15 > finish, begin + 15, finish)
-    jobs = (
-        (begin, first_column), (begin + 3, second_column), (begin + 14, rows_here),
-        (finish, solve_corner), (finish + 1, solve_second), (finish + 2, early_tiles),
-    )
+    slices = [functools.partial(unless_first, old_here, 0)]
+    slices += [functools.partial(unless_first, place, 0, r) for r in range(rb)]
+    for c in range(1, cb):
+        slices += [functools.partial(old_here, c)] + [functools.partial(place, c, r) for r in range(rb)]
+    jobs = [(begin + j, body) for j, body in enumerate(slices)]
+    jobs += [(begin + 14, rows_here), (finish, solve_corner), (finish + 1, solve_second), (finish + 2, early_tiles)]
 
     def step(i):
         @pl.when(jnp.logical_and(z != 0, i == turn))

time: 83.3 us -> 83.8 us (level)
  no operation moved by 1% of the time
where the time goes in v5:
time: 83.8 us; the launch traced here: 83.6 us
  Pallas kernels  80.5 us (96%)
  local copies, waits for them, and re-layouts  3.04 us (4%)
    pallas_call x1, Pallas kernels, shards(): pl.pallas_call(functools.partial(kernel, (rb, cb, nb, proc_rows, nz)), ou...  80.5 us
    unnamed x5, local copies, waits for them, and re-layouts  3.04 us

profile of v5, /device:TPU:305, one launch (start us, length us, event | category | flops | bytes accessed | tf_op | source)
XLA Modules:
  0.0 83.6 jit_solution(3917367508382799263)
XLA Ops:
  0.0 0.0 copy-start
  0.0 1.0 %copy-done = f32[2,256,256]{2,1,0:T(8,128)S(1)} copy-done((f32[2,256,256]{2,1,0:T(8,128)S(1)}, f32[2,256,256]{2,1,0:T(8,128)}, u32[]{:S(2)}) %copy-start) | copy-done | bytes 524312
  1.0 0.0 copy-start.1
  1.0 0.7 copy-done.1
  1.7 80.5 %shard_map.37 = f32[4,1,256,2,1,256]{5,4,3,2,1,0:T(1,128)S(1)} custom-call(f32[4,1,256,2,1,256]{5,4,3,2,1,0:T(1,128)} %x.1, s32[2,256]{1,0:T(2,128)S(1)} %copy-done.1, f32[2,256,256]{2,1,0:T(8,128)S(1)} %copy-done), custom_call_target="tpu_custom_call" | custom-call | tf_op jit(solution)/shard_map/pallas_call | solution.py:446
  82.3 1.3 %copy.5 = f32[4,1,256,2,1,256]{5,4,3,2,1,0:T(1,128)} copy(f32[4,1,256,2,1,256]{5,4,3,2,1,0:T(1,128)S(1)} %shard_map.37) | data formatting | bytes 4194304
Async XLA Ops:
  0.0 1.0 %copy-start = (f32[2,256,256]{2,1,0:T(8,128)S(1)}, f32[2,256,256]{2,1,0:T(8,128)}, u32[]{:S(2)}) copy-start(f32[2,256,256]{2,1,0:T(8,128)} %inv_in.1) | copy-start | bytes 1572868
  1.0 0.7 copy-start.1

commit v6 on v2

--- a/solution.py
+++ b/solution.py
@@ -90,10 +90,28 @@
             load(r, c).start()
     load_inv.start()
 
+    children = [[] for _ in range(nz)]
+    for sign, reach in ((1, middle), (-1, nz - middle - 1)):
+        for n in range(1, reach + 1):
+            parent = n - 2 if n % 2 == 0 else (n + 1 if n < reach else n - 1)
+            children[sign * parent % nz].insert(0, sign * n % nz)
+    partners = [children[zz] + [p for p in range(nz) if zz in children[p]] for zz in range(nz)]
+
     barrier = pltpu.get_barrier_semaphore()
     loop(1, np_, lambda d: pl.semaphore_signal(barrier, inc=1, device_id=at_row((me + d) % np_)))
-    for zz, cc in (((z + 1) % nz, core), ((z + nz - 1) % nz, core), (z, 1 - core)):
-        pl.semaphore_signal(barrier, inc=1, device_id=at_col(zz, cc))
+    pl.semaphore_signal(barrier, inc=1, device_id=at_col(z, 1 - core))
+
+    def with_partners(body):
+        for zz in range(nz):
+            @pl.when(z == zz)
+            def _():
+                body(partners[zz])
+
+    def greet_line(others):
+        for zz in others:
+            pl.semaphore_signal(barrier, inc=1, device_id=at_col(zz, core))
+
+    with_partners(greet_line)
 
     load_piv.wait()
     lane = lax.broadcasted_iota(jnp.int32, (nb, nb), 1)
@@ -221,22 +239,21 @@
         at = panel.at[1 - core, pl.ds(t * nb, nb), :]
         pltpu.make_async_remote_copy(at, at, sib_send, sib_recv.at[t], device_id=at_col(z, 1 - core)).wait_recv()
 
+    def pass_on(i):
+        for zz in range(nz):
+            if children[zz]:
+                @pl.when(z == zz)
+                def _():
+                    for child, sem in zip(children[zz], (z_send, z_send2)):
+                        z_copy(i, child, sem).start()
+
     def send(i):
-        z_copy(i, 1, z_send).start()
-        z_copy(i, nz - 1, z_send2).start()
+        pass_on(i)
         sib_copy(i).start()
 
     def relay(i):
         z_copy(i, z, z_send).wait_recv()
-
-        @pl.when(jnp.logical_and(z < middle, z > 0))
-        def _():
-            z_copy(i, z + 1, z_send).start()
-
-        @pl.when(z > middle + 1)
-        def _():
-            z_copy(i, z - 1, z_send).start()
-
+        pass_on(i)
         sib_copy(i).start()
 
     def tile(r):
@@ -308,7 +325,7 @@
             store(r, c).start()
 
     load(0, 0).wait()
-    pl.semaphore_wait(barrier, np_ - 1 + 3)
+    with_partners(lambda others: pl.semaphore_wait(barrier, np_ + len(others)))
     old_scatter(0)
     for r in range(1, rb):
         load(r, 0).wait()
@@ -424,13 +441,12 @@
 
     sent(sib_send)
 
-    @pl.when(jnp.logical_or(z < middle, z > middle + 1))
-    def _():
-        sent(z_send)
-
-    @pl.when(z == 0)
-    def _():
-        sent(z_send2)
+    for zz in range(nz):
+        if children[zz]:
+            @pl.when(z == zz)
+            def _():
+                for _, sem in zip(children[zz], (z_send, z_send2)):
+                    sent(sem)
 
     for r in range(rb):
         for c in range(cb):

time: 83.3 us -> 79.3 us (0.952)
  the two profiles are of different devices: /device:TPU:305 before, /device:TPU:241 now
where the time goes in v6:
time: 79.3 us; the launch traced here: 79.1 us
  Pallas kernels  76 us (96%)
  local copies, waits for them, and re-layouts  3.04 us (4%)
    pallas_call x1, Pallas kernels, shards(): pl.pallas_call(functools.partial(kernel, (rb, cb, nb, proc_rows, nz)), ou...  76 us
    unnamed x5, local copies, waits for them, and re-layouts  3.04 us

profile of v6, /device:TPU:241, one launch (start us, length us, event | category | flops | bytes accessed | tf_op | source)
XLA Modules:
  0.0 79.1 jit_solution(513147238094032073)
XLA Ops:
  0.0 0.0 copy-start
  0.0 1.0 %copy-done = f32[2,256,256]{2,1,0:T(8,128)S(1)} copy-done((f32[2,256,256]{2,1,0:T(8,128)S(1)}, f32[2,256,256]{2,1,0:T(8,128)}, u32[]{:S(2)}) %copy-start) | copy-done | bytes 524312
  1.0 0.0 copy-start.1
  1.0 0.7 copy-done.1
  1.7 76.0 %shard_map.37 = f32[4,1,256,2,1,256]{5,4,3,2,1,0:T(1,128)S(1)} custom-call(f32[4,1,256,2,1,256]{5,4,3,2,1,0:T(1,128)} %x.1, s32[2,256]{1,0:T(2,128)S(1)} %copy-done.1, f32[2,256,256]{2,1,0:T(8,128)S(1)} %copy-done), custom_call_target="tpu_custom_call" | custom-call | tf_op jit(solution)/shard_map/pallas_call | solution.py:465
  77.8 1.3 %copy.5 = f32[4,1,256,2,1,256]{5,4,3,2,1,0:T(1,128)} copy(f32[4,1,256,2,1,256]{5,4,3,2,1,0:T(1,128)S(1)} %shard_map.37) | data formatting | bytes 4194304
Async XLA Ops:
  0.0 1.0 %copy-start = (f32[2,256,256]{2,1,0:T(8,128)S(1)}, f32[2,256,256]{2,1,0:T(8,128)}, u32[]{:S(2)}) copy-start(f32[2,256,256]{2,1,0:T(8,128)} %inv_in.1) | copy-start | bytes 1572868
  1.0 0.7 copy-start.1
